TPU v7x, 32 devices: a whole 2x2x4 slice. The times are simulated.
32 devices in a mesh: groups: 2 (over y), gx: 4 (over z), gy: 2 (over x), gz: 2 (over core).
Axes of the slice: x: 2, y: 2, z: 4, core: 2. Of those that a mesh axis runs over, the one named last changes fastest.
Arguments:
- wave_state: float32 [18, 4, 64, 256], P('groups', 'gz', 'gx', 'gy'), parts along dimension 0, may hold values from -6 to 6
- buoyancy: float32 [8, 64, 256], P(('groups', 'gz'), 'gx', 'gy'), parts along dimension 0, may hold values from 0.5 to 2
- sponge_level: int32 [8, 64, 256], P(('groups', 'gz'), 'gx', 'gy'), parts along dimension 0, may hold values from 0 to 6, as said below
- spins: float32 [6, 8, 64, 256], P('groups', 'gz', 'gx', 'gy'), parts along dimension 0, as said below
- regions: int32 [128, 2], P(('groups', 'gx'), 'gy'), parts along dimension 0, may hold values from 0 to 3
- region_table: float32 [4, 4], replicated, may hold values from 0.3 to 1.5
Outputs:
- wave_out: float32 [18, 4, 64, 256], P('groups', 'gz', 'gx', 'gy'), parts along dimension 0
- spins_out: float32 [6, 8, 64, 256], P('groups', 'gz', 'gx', 'gy'), parts along dimension 0
There are 2 independent parts, one for each index of `groups`. A program takes and returns all parts, laid end to end along the dimension named above; an argument that names none is the same for every part. Nothing has to cross between parts.
Inputs may be any that keep to these rules, and one draw needn't show every extreme that they name: `sponge_level`: levels are highest at the lateral edges and fall inward. `spins`: each cell's three components form a vector of length one.
All inputs are finite; a program needn't handle non-finite values.
Results may differ from a plain program's by a relative error of at most 0.00026.
Values sent between devices are 32-bit elements; how exact they have to be, the bound alone decides.
A program may use at most 64 MiB of HBM per device.

v0:
```python
import jax
import jax.numpy as jnp
from jax import lax
from jax.sharding import PartitionSpec as P

TILE = 128
SUBSTEPS = 4
LLG_STEPS = 2


LAME_FIRST = 1.0
LAME_SHEAR = 1.0
ELASTIC_STEP = 0.3
SPIN_STEP = 0.04
DAMPING = 0.3
FORCE_SCALE = 0.25
SPONGE_RATE = 0.08
POISSON = LAME_FIRST / (3.0 * LAME_FIRST + 2.0 * LAME_SHEAR)


def with_halo(cells, sides, width):
    for axis, dim in sides:
        count = lax.axis_size(axis)
        ends = count - 1
        head = lax.slice_in_dim(cells, 0, width, axis=dim)
        tail = lax.slice_in_dim(cells, cells.shape[dim] - width, cells.shape[dim], axis=dim)
        cells = jnp.concatenate(
            [
                lax.ppermute(tail, axis, [(i, (i + 1) % count) for i in range(ends)]),
                cells,
                lax.ppermute(head, axis, [((i + 1) % count, i) for i in range(ends)]),
            ],
            axis=dim,
        )
    return cells


def from_root(array, axis, root):
    mine = lax.axis_index(axis) == root
    return lax.psum(jnp.where(mine, array, jnp.zeros_like(array)), axis)


def slope(extended, component, which_axis):
    field = extended[component]
    upper_cut = [slice(1, -1)] * 3
    lower_cut = [slice(1, -1)] * 3
    upper_cut[which_axis] = slice(2, None)
    lower_cut[which_axis] = slice(0, -2)
    return 0.5 * (field[tuple(upper_cut)] - field[tuple(lower_cut)])


def brick_stress(stresses):
    return with_halo(stresses, (("gx", 2), ("gy", 3), ("gz", 1)), 1)


def brick_velocity(velocity):
    return with_halo(velocity, (("gx", 2), ("gy", 3), ("gz", 1)), 1)


def elastic_step(
    velocity, stresses, buoyant, damping_factor, surface_force, widen_stress, widen_velocity
):
    wide_stress = widen_stress(stresses)

    def grad_stress(component, which_axis):
        return slope(wide_stress, component, which_axis)

    divergence = jnp.stack(
        [
            grad_stress(0, 1) + grad_stress(5, 2) + grad_stress(4, 0),
            grad_stress(5, 1) + grad_stress(1, 2) + grad_stress(3, 0),
            grad_stress(4, 1) + grad_stress(3, 2) + grad_stress(2, 0),
        ]
    )
    divergence = divergence.at[:, 0].add(surface_force)
    velocity = damping_factor * (velocity + ELASTIC_STEP * buoyant * divergence)
    wide_velocity = widen_velocity(velocity)

    def grad_velocity(component, which_axis):
        return slope(wide_velocity, component, which_axis)

    strain_xx = grad_velocity(0, 1)
    strain_yy = grad_velocity(1, 2)
    strain_zz = grad_velocity(2, 0)
    trace = strain_xx + strain_yy + strain_zz
    stress_rate = jnp.stack(
        [
            LAME_FIRST * trace + 2.0 * LAME_SHEAR * strain_xx,
            LAME_FIRST * trace + 2.0 * LAME_SHEAR * strain_yy,
            LAME_FIRST * trace + 2.0 * LAME_SHEAR * strain_zz,
            LAME_SHEAR * (grad_velocity(1, 0) + grad_velocity(2, 2)),
            LAME_SHEAR * (grad_velocity(0, 0) + grad_velocity(2, 1)),
            LAME_SHEAR * (grad_velocity(0, 2) + grad_velocity(1, 1)),
        ]
    )
    stresses = damping_factor * (stresses + ELASTIC_STEP * stress_rate)
    return (velocity, stresses)


def spin_step(extended, surface, anisotropy, chirality, normal_couple, shear_couple):
    centre = extended[:, 1:-1, 1:-1, 1:-1]
    laplace = (
        extended[:, 2:, 1:-1, 1:-1]
        + extended[:, :-2, 1:-1, 1:-1]
        + extended[:, 1:-1, 2:, 1:-1]
        + extended[:, 1:-1, :-2, 1:-1]
        + extended[:, 1:-1, 1:-1, 2:]
        + extended[:, 1:-1, 1:-1, :-2]
        - 6.0 * centre
    )
    along_x = 0.5 * (extended[:, 1:-1, 2:, 1:-1] - extended[:, 1:-1, :-2, 1:-1])
    along_y = 0.5 * (extended[:, 1:-1, 1:-1, 2:] - extended[:, 1:-1, 1:-1, :-2])
    trace = surface[0] + surface[1] + surface[2]
    strain_xx = (surface[0] - POISSON * trace) / (2.0 * LAME_SHEAR)
    strain_yy = (surface[1] - POISSON * trace) / (2.0 * LAME_SHEAR)
    strain_zz = (surface[2] - POISSON * trace) / (2.0 * LAME_SHEAR)
    strain_yz = surface[3] / (2.0 * LAME_SHEAR)
    strain_xz = surface[4] / (2.0 * LAME_SHEAR)
    strain_xy = surface[5] / (2.0 * LAME_SHEAR)
    spin_x, spin_y, spin_z = (centre[0], centre[1], centre[2])
    coupled_x = -2.0 * normal_couple * strain_xx * spin_x - 2.0 * shear_couple * (
        strain_xy * spin_y + strain_xz * spin_z
    )
    coupled_y = -2.0 * normal_couple * strain_yy * spin_y - 2.0 * shear_couple * (
        strain_xy * spin_x + strain_yz * spin_z
    )
    coupled_z = -2.0 * normal_couple * strain_zz * spin_z - 2.0 * shear_couple * (
        strain_xz * spin_x + strain_yz * spin_y
    )
    field_x = laplace[0] + chirality * along_x[2] + coupled_x
    field_y = laplace[1] + chirality * along_y[2] + coupled_y
    field_z = (
        laplace[2] - chirality * (along_x[0] + along_y[1]) + 2.0 * anisotropy * spin_z + coupled_z
    )
    torque_x = spin_y * field_z - spin_z * field_y
    torque_y = spin_z * field_x - spin_x * field_z
    torque_z = spin_x * field_y - spin_y * field_x
    relax_x = spin_y * torque_z - spin_z * torque_y
    relax_y = spin_z * torque_x - spin_x * torque_z
    relax_z = spin_x * torque_y - spin_y * torque_x
    factor = SPIN_STEP / (1.0 + DAMPING * DAMPING)
    moved = jnp.stack(
        [
            spin_x - factor * (torque_x + DAMPING * relax_x),
            spin_y - factor * (torque_y + DAMPING * relax_y),
            spin_z - factor * (torque_z + DAMPING * relax_z),
        ]
    )
    length_now = jnp.sqrt(moved[0] * moved[0] + moved[1] * moved[1] + moved[2] * moved[2])
    return moved / length_now


def film_push(film_spins, normal_couple, shear_couple):
    spin_x, spin_y, spin_z = (film_spins[0], film_spins[1], film_spins[2])
    return FORCE_SCALE * jnp.stack(
        [
            shear_couple * jnp.sum(spin_x * spin_z, axis=0),
            shear_couple * jnp.sum(spin_y * spin_z, axis=0),
            normal_couple * jnp.sum(spin_z * spin_z - 1.0 / 3.0, axis=0),
        ]
    )


def mend(extended, which_axis, at_low, at_high):
    extent = extended.shape[which_axis]
    low_out = lax.slice_in_dim(extended, 0, 1, axis=which_axis)
    low_in = lax.slice_in_dim(extended, 1, 2, axis=which_axis)
    middle = lax.slice_in_dim(extended, 1, extent - 1, axis=which_axis)
    high_in = lax.slice_in_dim(extended, extent - 2, extent - 1, axis=which_axis)
    high_out = lax.slice_in_dim(extended, extent - 1, extent, axis=which_axis)
    return jnp.concatenate(
        [jnp.where(at_low, low_in, low_out), middle, jnp.where(at_high, high_in, high_out)],
        axis=which_axis,
    )


def material_of(regions, region_table):
    region_ids = jnp.arange(region_table.shape[1], dtype=jnp.int32)
    one_hot = (regions[None] == region_ids[:, None, None]).astype(jnp.float32)
    per_tile = jnp.einsum("pr,rxt->pxt", region_table, one_hot, precision=lax.Precision.HIGHEST)
    rows_here = regions.shape[0]
    tile_count = regions.shape[1]
    spread_out = jnp.broadcast_to(per_tile[:, :, :, None], (4, rows_here, tile_count, TILE))
    return spread_out.reshape(4, rows_here, tile_count * TILE)


def body(wave_state, buoyancy, sponge_level, spins, regions, region_table):
    damping_factor = 1.0 - SPONGE_RATE * sponge_level.astype(jnp.float32)
    material = material_of(regions, region_table)
    layer_first = lax.axis_index("gz") == 0
    layer_last = lax.axis_index("gz") == lax.axis_size("gz") - 1
    x_first = lax.axis_index("gx") == 0
    x_last = lax.axis_index("gx") == lax.axis_size("gx") - 1
    y_first = lax.axis_index("gy") == 0
    y_last = lax.axis_index("gy") == lax.axis_size("gy") - 1
    wave_now = wave_state
    top_flag = layer_first.astype(jnp.float32)
    velocity, stresses = (wave_now[:3], wave_now[3:])
    film_spins = spins
    for llg_step in range(LLG_STEPS):
        surface = from_root(stresses[:, 0], "gz", 0)
        extended = with_halo(film_spins, (("gx", 2), ("gy", 3), ("gz", 1)), 1)
        extended = mend(extended, 1, layer_first, layer_last)
        extended = mend(extended, 2, x_first, x_last)
        extended = mend(extended, 3, y_first, y_last)
        film_spins = spin_step(
            extended, surface, material[0], material[1], material[2], material[3]
        )
        layer_sum = film_push(film_spins, material[2], material[3])
        surface_force = lax.psum(layer_sum, "gz")
        surface_force = surface_force * top_flag
        for sub_step in range(SUBSTEPS):
            velocity, stresses = elastic_step(
                velocity,
                stresses,
                buoyancy,
                damping_factor,
                surface_force,
                brick_stress,
                brick_velocity,
            )
    wave_now = jnp.concatenate([velocity, stresses], axis=0)
    return (wave_now, film_spins)


def solution(mesh):
    return jax.shard_map(
        body,
        mesh=mesh,
        in_specs=(
            P("groups", "gz", "gx", "gy"),
            P(("groups", "gz"), "gx", "gy"),
            P(("groups", "gz"), "gx", "gy"),
            P("groups", "gz", "gx", "gy"),
            P(("groups", "gx"), "gy"),
            P(),
        ),
        out_specs=(P("groups", "gz", "gx", "gy"), P("groups", "gz", "gx", "gy")),
        check_vma=False,
    )
```

profile of v0, /device:TPU:0, one launch (start us, length us, event | category | flops | bytes accessed | tf_op | source)
XLA Modules:
  0.0 391.9 jit_solution(16700243618656175618)
XLA Ops:
  2.8 5.6 %collective-permute-start = (f32[6,2,1,128]{3,2,1,0:T(1,128)S(1)}, f32[6,2,1,128]{3,2,1,0:T(1,128)S(1)}, u32[]{:S(2)}, u32[]{:S(2)}) collective-permute-start(f32[6,2,1,128]{3,2,1,0:T(1,128)S(1)} %get-tuple-element.280), channel_id=1, source_target_pairs={{0,4},{4,8},{8,12},{1,5},{5,9},{9,13},{2,6},{6,10},{10,14},{3,7},{... | collective-permute-start | bytes 18440 | tf_op jit(solution)/shard_map/ppermute | solution.py:29
  10.5 4.6 %collective-permute-start.6 = (f32[3,4,1,128]{3,2,1,0:T(1,128)S(1)}, f32[3,4,1,128]{3,2,1,0:T(1,128)S(1)}, u32[]{:S(2)}, u32[]{:S(2)}) collective-permute-start(f32[3,4,1,128]{3,2,1,0:T(1,128)S(1)} %get-tuple-element.319), channel_id=1, source_target_pairs={{0,4},{4,8},{8,12},{1,5},{5,9},{9,13},{2,6},{6,10},{10,14},{3,7},{... | collective-permute-start | bytes 18440 | tf_op jit(solution)/shard_map/ppermute | solution.py:29
  23.5 4.6 %collective-permute-start.8 = (f32[3,4,18,1]{3,2,1,0:T(8,128)S(1)}, f32[3,4,18,1]{3,2,1,0:T(8,128)S(1)}, u32[]{:S(2)}, u32[]{:S(2)}) collective-permute-start(f32[3,4,18,1]{3,2,1,0:T(8,128)S(1)} %get-tuple-element.276), channel_id=1, source_target_pairs={{0,2},{1,3},{4,6},{5,7},{8,10},{9,11},{12,14},{13,15},{16,18},{17,... | collective-permute-start | bytes 2600 | tf_op jit(solution)/shard_map/ppermute | solution.py:29
  29.6 4.6 %collective-permute-start.2 = (f32[6,2,18,1]{3,2,1,0:T(8,128)S(1)}, f32[6,2,18,1]{3,2,1,0:T(8,128)S(1)}, u32[]{:S(2)}, u32[]{:S(2)}) collective-permute-start(f32[6,2,18,1]{3,2,1,0:T(8,128)S(1)} %get-tuple-element.278), channel_id=1, source_target_pairs={{0,2},{1,3},{4,6},{5,7},{8,10},{9,11},{12,14},{13,15},{16,18},{17,... | collective-permute-start | bytes 2600 | tf_op jit(solution)/shard_map/ppermute | solution.py:29
  71.5 4.8 %collective-permute-start.18 = (f32[6,2,1,128]{3,2,1,0:T(1,128)S(1)}, f32[6,2,1,128]{3,2,1,0:T(1,128)S(1)}, u32[]{:S(2)}, u32[]{:S(2)}) collective-permute-start(f32[6,2,1,128]{3,2,1,0:T(1,128)S(1)} %get-tuple-element.317), channel_id=1, source_target_pairs={{0,4},{4,8},{8,12},{1,5},{5,9},{9,13},{2,6},{6,10},{10,14},{3,7},{... | collective-permute-start | bytes 18440 | tf_op jit(solution)/shard_map/ppermute | solution.py:29
  79.1 4.6 %collective-permute-start.20 = (f32[6,2,18,1]{3,2,1,0:T(8,128)S(1)}, f32[6,2,18,1]{3,2,1,0:T(8,128)S(1)}, u32[]{:S(2)}, u32[]{:S(2)}) collective-permute-start(f32[6,2,18,1]{3,2,1,0:T(8,128)S(1)} %get-tuple-element.272), channel_id=1, source_target_pairs={{0,2},{1,3},{4,6},{5,7},{8,10},{9,11},{12,14},{13,15},{16,18},{17,... | collective-permute-start | bytes 2600 | tf_op jit(solution)/shard_map/ppermute | solution.py:29
  93.7 4.8 %collective-permute-start.24 = (f32[3,2,1,128]{3,2,1,0:T(1,128)S(1)}, f32[3,2,1,128]{3,2,1,0:T(1,128)S(1)}, u32[]{:S(2)}, u32[]{:S(2)}) collective-permute-start(f32[3,2,1,128]{3,2,1,0:T(1,128)S(1)} %get-tuple-element.359), channel_id=1, source_target_pairs={{0,4},{4,8},{8,12},{1,5},{5,9},{9,13},{2,6},{6,10},{10,14},{3,7},{... | collective-permute-start | bytes 9224 | tf_op jit(solution)/shard_map/ppermute | solution.py:29
  107.1 4.8 %collective-permute-start.60 = (f32[3,4,1,128]{3,2,1,0:T(1,128)S(1)}, f32[3,4,1,128]{3,2,1,0:T(1,128)S(1)}, u32[]{:S(2)}, u32[]{:S(2)}) collective-permute-start(f32[3,4,1,128]{3,2,1,0:T(1,128)S(1)} %get-tuple-element.297), channel_id=1, source_target_pairs={{0,4},{4,8},{8,12},{1,5},{5,9},{9,13},{2,6},{6,10},{10,14},{3,7},{... | collective-permute-start | bytes 18440 | tf_op jit(solution)/shard_map/ppermute | solution.py:29
  125.4 4.6 %collective-permute-start.62 = (f32[3,4,18,1]{3,2,1,0:T(8,128)S(1)}, f32[3,4,18,1]{3,2,1,0:T(8,128)S(1)}, u32[]{:S(2)}, u32[]{:S(2)}) collective-permute-start(f32[3,4,18,1]{3,2,1,0:T(8,128)S(1)} %get-tuple-element.258), channel_id=1, source_target_pairs={{0,2},{1,3},{4,6},{5,7},{8,10},{9,11},{12,14},{13,15},{16,18},{17,... | collective-permute-start | bytes 2600 | tf_op jit(solution)/shard_map/ppermute | solution.py:29
  131.4 4.6 %collective-permute-start.32 = (f32[6,2,18,1]{3,2,1,0:T(8,128)S(1)}, f32[6,2,18,1]{3,2,1,0:T(8,128)S(1)}, u32[]{:S(2)}, u32[]{:S(2)}) collective-permute-start(f32[6,2,18,1]{3,2,1,0:T(8,128)S(1)} %get-tuple-element.268), channel_id=1, source_target_pairs={{0,2},{1,3},{4,6},{5,7},{8,10},{9,11},{12,14},{13,15},{16,18},{17,... | collective-permute-start | bytes 2600 | tf_op jit(solution)/shard_map/ppermute | solution.py:29
  167.7 4.8 %collective-permute-start.42 = (f32[6,2,1,128]{3,2,1,0:T(1,128)S(1)}, f32[6,2,1,128]{3,2,1,0:T(1,128)S(1)}, u32[]{:S(2)}, u32[]{:S(2)}) collective-permute-start(f32[6,2,1,128]{3,2,1,0:T(1,128)S(1)} %get-tuple-element.307), channel_id=1, source_target_pairs={{0,4},{4,8},{8,12},{1,5},{5,9},{9,13},{2,6},{6,10},{10,14},{3,7},{... | collective-permute-start | bytes 18440 | tf_op jit(solution)/shard_map/ppermute | solution.py:29
  175.3 4.6 %collective-permute-start.44 = (f32[6,2,18,1]{3,2,1,0:T(8,128)S(1)}, f32[6,2,18,1]{3,2,1,0:T(8,128)S(1)}, u32[]{:S(2)}, u32[]{:S(2)}) collective-permute-start(f32[6,2,18,1]{3,2,1,0:T(8,128)S(1)} %get-tuple-element.264), channel_id=1, source_target_pairs={{0,2},{1,3},{4,6},{5,7},{8,10},{9,11},{12,14},{13,15},{16,18},{17,... | collective-permute-start | bytes 2600 | tf_op jit(solution)/shard_map/ppermute | solution.py:29
  189.9 4.8 %collective-permute-start.48 = (f32[3,2,1,128]{3,2,1,0:T(1,128)S(1)}, f32[3,2,1,128]{3,2,1,0:T(1,128)S(1)}, u32[]{:S(2)}, u32[]{:S(2)}) collective-permute-start(f32[3,2,1,128]{3,2,1,0:T(1,128)S(1)} %get-tuple-element.355), channel_id=1, source_target_pairs={{0,4},{4,8},{8,12},{1,5},{5,9},{9,13},{2,6},{6,10},{10,14},{3,7},{... | collective-permute-start | bytes 9224 | tf_op jit(solution)/shard_map/ppermute | solution.py:29
  211.6 4.8 %collective-permute-start.54 = (f32[6,2,1,128]{3,2,1,0:T(1,128)S(1)}, f32[6,2,1,128]{3,2,1,0:T(1,128)S(1)}, u32[]{:S(2)}, u32[]{:S(2)}) collective-permute-start(f32[6,2,1,128]{3,2,1,0:T(1,128)S(1)} %get-tuple-element.302), channel_id=1, source_target_pairs={{0,4},{4,8},{8,12},{1,5},{5,9},{9,13},{2,6},{6,10},{10,14},{3,7},{... | collective-permute-start | bytes 18440 | tf_op jit(solution)/shard_map/ppermute | solution.py:29
  222.4 4.6 %collective-permute-start.56 = (f32[6,2,18,1]{3,2,1,0:T(8,128)S(1)}, f32[6,2,18,1]{3,2,1,0:T(8,128)S(1)}, u32[]{:S(2)}, u32[]{:S(2)}) collective-permute-start(f32[6,2,18,1]{3,2,1,0:T(8,128)S(1)} %get-tuple-element.260), channel_id=1, source_target_pairs={{0,2},{1,3},{4,6},{5,7},{8,10},{9,11},{12,14},{13,15},{16,18},{17,... | collective-permute-start | bytes 2600 | tf_op jit(solution)/shard_map/ppermute | solution.py:29
  261.4 4.8 %collective-permute-start.72 = (f32[6,2,1,128]{3,2,1,0:T(1,128)S(1)}, f32[6,2,1,128]{3,2,1,0:T(1,128)S(1)}, u32[]{:S(2)}, u32[]{:S(2)}) collective-permute-start(f32[6,2,1,128]{3,2,1,0:T(1,128)S(1)} %get-tuple-element.295), channel_id=1, source_target_pairs={{0,4},{4,8},{8,12},{1,5},{5,9},{9,13},{2,6},{6,10},{10,14},{3,7},{... | collective-permute-start | bytes 18440 | tf_op jit(solution)/shard_map/ppermute | solution.py:29
  269.0 4.6 %collective-permute-start.74 = (f32[6,2,18,1]{3,2,1,0:T(8,128)S(1)}, f32[6,2,18,1]{3,2,1,0:T(8,128)S(1)}, u32[]{:S(2)}, u32[]{:S(2)}) collective-permute-start(f32[6,2,18,1]{3,2,1,0:T(8,128)S(1)} %get-tuple-element.254), channel_id=1, source_target_pairs={{0,2},{1,3},{4,6},{5,7},{8,10},{9,11},{12,14},{13,15},{16,18},{17,... | collective-permute-start | bytes 2600 | tf_op jit(solution)/shard_map/ppermute | solution.py:29
  283.6 4.8 %collective-permute-start.78 = (f32[3,2,1,128]{3,2,1,0:T(1,128)S(1)}, f32[3,2,1,128]{3,2,1,0:T(1,128)S(1)}, u32[]{:S(2)}, u32[]{:S(2)}) collective-permute-start(f32[3,2,1,128]{3,2,1,0:T(1,128)S(1)} %get-tuple-element.348), channel_id=1, source_target_pairs={{0,4},{4,8},{8,12},{1,5},{5,9},{9,13},{2,6},{6,10},{10,14},{3,7},{... | collective-permute-start | bytes 9224 | tf_op jit(solution)/shard_map/ppermute | solution.py:29
  305.1 4.8 %collective-permute-start.84 = (f32[6,2,1,128]{3,2,1,0:T(1,128)S(1)}, f32[6,2,1,128]{3,2,1,0:T(1,128)S(1)}, u32[]{:S(2)}, u32[]{:S(2)}) collective-permute-start(f32[6,2,1,128]{3,2,1,0:T(1,128)S(1)} %get-tuple-element.290), channel_id=1, source_target_pairs={{0,4},{4,8},{8,12},{1,5},{5,9},{9,13},{2,6},{6,10},{10,14},{3,7},{... | collective-permute-start | bytes 18440 | tf_op jit(solution)/shard_map/ppermute | solution.py:29
  312.7 4.6 %collective-permute-start.86 = (f32[6,2,18,1]{3,2,1,0:T(8,128)S(1)}, f32[6,2,18,1]{3,2,1,0:T(8,128)S(1)}, u32[]{:S(2)}, u32[]{:S(2)}) collective-permute-start(f32[6,2,18,1]{3,2,1,0:T(8,128)S(1)} %get-tuple-element.250), channel_id=1, source_target_pairs={{0,2},{1,3},{4,6},{5,7},{8,10},{9,11},{12,14},{13,15},{16,18},{17,... | collective-permute-start | bytes 2600 | tf_op jit(solution)/shard_map/ppermute | solution.py:29
  327.3 4.8 %collective-permute-start.90 = (f32[3,2,1,128]{3,2,1,0:T(1,128)S(1)}, f32[3,2,1,128]{3,2,1,0:T(1,128)S(1)}, u32[]{:S(2)}, u32[]{:S(2)}) collective-permute-start(f32[3,2,1,128]{3,2,1,0:T(1,128)S(1)} %get-tuple-element.346), channel_id=1, source_target_pairs={{0,4},{4,8},{8,12},{1,5},{5,9},{9,13},{2,6},{6,10},{10,14},{3,7},{... | collective-permute-start | bytes 9224 | tf_op jit(solution)/shard_map/ppermute | solution.py:29
  348.8 4.8 %collective-permute-start.96 = (f32[6,2,1,128]{3,2,1,0:T(1,128)S(1)}, f32[6,2,1,128]{3,2,1,0:T(1,128)S(1)}, u32[]{:S(2)}, u32[]{:S(2)}) collective-permute-start(f32[6,2,1,128]{3,2,1,0:T(1,128)S(1)} %get-tuple-element.285), channel_id=1, source_target_pairs={{0,4},{4,8},{8,12},{1,5},{5,9},{9,13},{2,6},{6,10},{10,14},{3,7},{... | collective-permute-start | bytes 18440 | tf_op jit(solution)/shard_map/ppermute | solution.py:29
  356.4 4.6 %collective-permute-start.98 = (f32[6,2,18,1]{3,2,1,0:T(8,128)S(1)}, f32[6,2,18,1]{3,2,1,0:T(8,128)S(1)}, u32[]{:S(2)}, u32[]{:S(2)}) collective-permute-start(f32[6,2,18,1]{3,2,1,0:T(8,128)S(1)} %get-tuple-element.246), channel_id=1, source_target_pairs={{0,2},{1,3},{4,6},{5,7},{8,10},{9,11},{12,14},{13,15},{16,18},{17,... | collective-permute-start | bytes 2600 | tf_op jit(solution)/shard_map/ppermute | solution.py:29
  371.0 4.8 %collective-permute-start.102 = (f32[3,2,1,128]{3,2,1,0:T(1,128)S(1)}, f32[3,2,1,128]{3,2,1,0:T(1,128)S(1)}, u32[]{:S(2)}, u32[]{:S(2)}) collective-permute-start(f32[3,2,1,128]{3,2,1,0:T(1,128)S(1)} %get-tuple-element.344), channel_id=1, source_target_pairs={{0,4},{4,8},{8,12},{1,5},{5,9},{9,13},{2,6},{6,10},{10,14},{3,7},{... | collective-permute-start | bytes 9224 | tf_op jit(solution)/shard_map/ppermute | solution.py:29
  (467 shorter events, 274.9 us)
Async XLA Ops:
  1.5 26.6 %collective-permute-start.1 = (f32[6,2,1,128]{3,2,1,0:T(1,128)S(1)}, f32[6,2,1,128]{3,2,1,0:T(1,128)S(1)}, u32[]{:S(2)}, u32[]{:S(2)}) collective-permute-start(f32[6,2,1,128]{3,2,1,0:T(1,128)S(1)} %get-tuple-element.281), channel_id=1, source_target_pairs={{4,0},{8,4},{12,8},{5,1},{9,5},{13,9},{6,2},{10,6},{14,10},{7,3},{... | collective-permute-start | bytes 18440 | tf_op jit(solution)/shard_map/ppermute | solution.py:31
  2.8 25.3 %collective-permute-start = (f32[6,2,1,128]{3,2,1,0:T(1,128)S(1)}, f32[6,2,1,128]{3,2,1,0:T(1,128)S(1)}, u32[]{:S(2)}, u32[]{:S(2)}) collective-permute-start(f32[6,2,1,128]{3,2,1,0:T(1,128)S(1)} %get-tuple-element.280), channel_id=1, source_target_pairs={{0,4},{4,8},{8,12},{1,5},{5,9},{9,13},{2,6},{6,10},{10,14},{3,7},{... | collective-permute-start | bytes 18440 | tf_op jit(solution)/shard_map/ppermute | solution.py:29
  9.2 12.1 %collective-permute-start.7 = (f32[3,4,1,128]{3,2,1,0:T(1,128)S(1)}, f32[3,4,1,128]{3,2,1,0:T(1,128)S(1)}, u32[]{:S(2)}, u32[]{:S(2)}) collective-permute-start(f32[3,4,1,128]{3,2,1,0:T(1,128)S(1)} %get-tuple-element.320), channel_id=1, source_target_pairs={{4,0},{8,4},{12,8},{5,1},{9,5},{13,9},{6,2},{10,6},{14,10},{7,3},{... | collective-permute-start | bytes 18440 | tf_op jit(solution)/shard_map/ppermute | solution.py:31
  10.5 10.8 %collective-permute-start.6 = (f32[3,4,1,128]{3,2,1,0:T(1,128)S(1)}, f32[3,4,1,128]{3,2,1,0:T(1,128)S(1)}, u32[]{:S(2)}, u32[]{:S(2)}) collective-permute-start(f32[3,4,1,128]{3,2,1,0:T(1,128)S(1)} %get-tuple-element.319), channel_id=1, source_target_pairs={{0,4},{4,8},{8,12},{1,5},{5,9},{9,13},{2,6},{6,10},{10,14},{3,7},{... | collective-permute-start | bytes 18440 | tf_op jit(solution)/shard_map/ppermute | solution.py:29
  22.2 11.9 %collective-permute-start.9 = (f32[3,4,18,1]{3,2,1,0:T(8,128)S(1)}, f32[3,4,18,1]{3,2,1,0:T(8,128)S(1)}, u32[]{:S(2)}, u32[]{:S(2)}) collective-permute-start(f32[3,4,18,1]{3,2,1,0:T(8,128)S(1)} %get-tuple-element.277), channel_id=1, source_target_pairs={{2,0},{3,1},{6,4},{7,5},{10,8},{11,9},{14,12},{15,13},{18,16},{19,... | collective-permute-start | bytes 2600 | tf_op jit(solution)/shard_map/ppermute | solution.py:31
  23.5 10.6 %collective-permute-start.8 = (f32[3,4,18,1]{3,2,1,0:T(8,128)S(1)}, f32[3,4,18,1]{3,2,1,0:T(8,128)S(1)}, u32[]{:S(2)}, u32[]{:S(2)}) collective-permute-start(f32[3,4,18,1]{3,2,1,0:T(8,128)S(1)} %get-tuple-element.276), channel_id=1, source_target_pairs={{0,2},{1,3},{4,6},{5,7},{8,10},{9,11},{12,14},{13,15},{16,18},{17,... | collective-permute-start | bytes 2600 | tf_op jit(solution)/shard_map/ppermute | solution.py:29
  28.3 7.4 %collective-permute-start.3 = (f32[6,2,18,1]{3,2,1,0:T(8,128)S(1)}, f32[6,2,18,1]{3,2,1,0:T(8,128)S(1)}, u32[]{:S(2)}, u32[]{:S(2)}) collective-permute-start(f32[6,2,18,1]{3,2,1,0:T(8,128)S(1)} %get-tuple-element.279), channel_id=1, source_target_pairs={{2,0},{3,1},{6,4},{7,5},{10,8},{11,9},{14,12},{15,13},{18,16},{19,... | collective-permute-start | bytes 2600 | tf_op jit(solution)/shard_map/ppermute | solution.py:31
  29.6 7.3 %collective-permute-start.2 = (f32[6,2,18,1]{3,2,1,0:T(8,128)S(1)}, f32[6,2,18,1]{3,2,1,0:T(8,128)S(1)}, u32[]{:S(2)}, u32[]{:S(2)}) collective-permute-start(f32[6,2,18,1]{3,2,1,0:T(8,128)S(1)} %get-tuple-element.278), channel_id=1, source_target_pairs={{0,2},{1,3},{4,6},{5,7},{8,10},{9,11},{12,14},{13,15},{16,18},{17,... | collective-permute-start | bytes 2600 | tf_op jit(solution)/shard_map/ppermute | solution.py:29
  79.1 7.2 %collective-permute-start.20 = (f32[6,2,18,1]{3,2,1,0:T(8,128)S(1)}, f32[6,2,18,1]{3,2,1,0:T(8,128)S(1)}, u32[]{:S(2)}, u32[]{:S(2)}) collective-permute-start(f32[6,2,18,1]{3,2,1,0:T(8,128)S(1)} %get-tuple-element.272), channel_id=1, source_target_pairs={{0,2},{1,3},{4,6},{5,7},{8,10},{9,11},{12,14},{13,15},{16,18},{17,... | collective-permute-start | bytes 2600 | tf_op jit(solution)/shard_map/ppermute | solution.py:29
  99.9 12.0 %collective-permute-start.27 = (f32[3,2,18,1]{3,2,1,0:T(8,128)S(1)}, f32[3,2,18,1]{3,2,1,0:T(8,128)S(1)}, u32[]{:S(2)}, u32[]{:S(2)}) collective-permute-start(f32[3,2,18,1]{3,2,1,0:T(8,128)S(1)} %get-tuple-element.337), channel_id=1, source_target_pairs={{2,0},{3,1},{6,4},{7,5},{10,8},{11,9},{14,12},{15,13},{18,16},{19,... | collective-permute-start | bytes 1304 | tf_op jit(solution)/shard_map/ppermute | solution.py:31
  101.2 10.7 %collective-permute-start.26 = (f32[3,2,18,1]{3,2,1,0:T(8,128)S(1)}, f32[3,2,18,1]{3,2,1,0:T(8,128)S(1)}, u32[]{:S(2)}, u32[]{:S(2)}) collective-permute-start(f32[3,2,18,1]{3,2,1,0:T(8,128)S(1)} %get-tuple-element.336), channel_id=1, source_target_pairs={{0,2},{1,3},{4,6},{5,7},{8,10},{9,11},{12,14},{13,15},{16,18},{17,... | collective-permute-start | bytes 1304 | tf_op jit(solution)/shard_map/ppermute | solution.py:29
  105.8 10.7 %collective-permute-start.61 = (f32[3,4,1,128]{3,2,1,0:T(1,128)S(1)}, f32[3,4,1,128]{3,2,1,0:T(1,128)S(1)}, u32[]{:S(2)}, u32[]{:S(2)}) collective-permute-start(f32[3,4,1,128]{3,2,1,0:T(1,128)S(1)} %get-tuple-element.298), channel_id=1, source_target_pairs={{4,0},{8,4},{12,8},{5,1},{9,5},{13,9},{6,2},{10,6},{14,10},{7,3},{... | collective-permute-start | bytes 18440 | tf_op jit(solution)/shard_map/ppermute | solution.py:31
  107.1 9.4 %collective-permute-start.60 = (f32[3,4,1,128]{3,2,1,0:T(1,128)S(1)}, f32[3,4,1,128]{3,2,1,0:T(1,128)S(1)}, u32[]{:S(2)}, u32[]{:S(2)}) collective-permute-start(f32[3,4,1,128]{3,2,1,0:T(1,128)S(1)} %get-tuple-element.297), channel_id=1, source_target_pairs={{0,4},{4,8},{8,12},{1,5},{5,9},{9,13},{2,6},{6,10},{10,14},{3,7},{... | collective-permute-start | bytes 18440 | tf_op jit(solution)/shard_map/ppermute | solution.py:29
  118.1 11.8 %collective-permute-start.31 = (f32[6,2,1,128]{3,2,1,0:T(1,128)S(1)}, f32[6,2,1,128]{3,2,1,0:T(1,128)S(1)}, u32[]{:S(2)}, u32[]{:S(2)}) collective-permute-start(f32[6,2,1,128]{3,2,1,0:T(1,128)S(1)} %get-tuple-element.313), channel_id=1, source_target_pairs={{4,0},{8,4},{12,8},{5,1},{9,5},{13,9},{6,2},{10,6},{14,10},{7,3},{... | collective-permute-start | bytes 18440 | tf_op jit(solution)/shard_map/ppermute | solution.py:31
  119.4 10.5 %collective-permute-start.30 = (f32[6,2,1,128]{3,2,1,0:T(1,128)S(1)}, f32[6,2,1,128]{3,2,1,0:T(1,128)S(1)}, u32[]{:S(2)}, u32[]{:S(2)}) collective-permute-start(f32[6,2,1,128]{3,2,1,0:T(1,128)S(1)} %get-tuple-element.312), channel_id=1, source_target_pairs={{0,4},{4,8},{8,12},{1,5},{5,9},{9,13},{2,6},{6,10},{10,14},{3,7},{... | collective-permute-start | bytes 18440 | tf_op jit(solution)/shard_map/ppermute | solution.py:29
  124.1 11.9 %collective-permute-start.63 = (f32[3,4,18,1]{3,2,1,0:T(8,128)S(1)}, f32[3,4,18,1]{3,2,1,0:T(8,128)S(1)}, u32[]{:S(2)}, u32[]{:S(2)}) collective-permute-start(f32[3,4,18,1]{3,2,1,0:T(8,128)S(1)} %get-tuple-element.259), channel_id=1, source_target_pairs={{2,0},{3,1},{6,4},{7,5},{10,8},{11,9},{14,12},{15,13},{18,16},{19,... | collective-permute-start | bytes 2600 | tf_op jit(solution)/shard_map/ppermute | solution.py:31
  125.4 10.6 %collective-permute-start.62 = (f32[3,4,18,1]{3,2,1,0:T(8,128)S(1)}, f32[3,4,18,1]{3,2,1,0:T(8,128)S(1)}, u32[]{:S(2)}, u32[]{:S(2)}) collective-permute-start(f32[3,4,18,1]{3,2,1,0:T(8,128)S(1)} %get-tuple-element.258), channel_id=1, source_target_pairs={{0,2},{1,3},{4,6},{5,7},{8,10},{9,11},{12,14},{13,15},{16,18},{17,... | collective-permute-start | bytes 2600 | tf_op jit(solution)/shard_map/ppermute | solution.py:29
  130.1 7.3 %collective-permute-start.33 = (f32[6,2,18,1]{3,2,1,0:T(8,128)S(1)}, f32[6,2,18,1]{3,2,1,0:T(8,128)S(1)}, u32[]{:S(2)}, u32[]{:S(2)}) collective-permute-start(f32[6,2,18,1]{3,2,1,0:T(8,128)S(1)} %get-tuple-element.269), channel_id=1, source_target_pairs={{2,0},{3,1},{6,4},{7,5},{10,8},{11,9},{14,12},{15,13},{18,16},{19,... | collective-permute-start | bytes 2600 | tf_op jit(solution)/shard_map/ppermute | solution.py:31
  143.4 7.7 %collective-permute-start.64 = (f32[3,1,18,130]{3,2,1,0:T(8,128)S(1)}, f32[3,1,18,130]{3,2,1,0:T(8,128)S(1)}, u32[]{:S(2)}, u32[]{:S(2)}) collective-permute-start(f32[3,1,18,130]{3,2,1,0:T(8,128)S(1)} %get-tuple-element.125), channel_id=1, source_target_pairs={{1,0},{3,2},{5,4},{7,6},{9,8},{11,10},{13,12},{15,14},{17,16},{19,... | collective-permute-start | bytes 84248 | tf_op jit(solution)/shard_map/ppermute | solution.py:31
  210.3 10.1 %collective-permute-start.55 = (f32[6,2,1,128]{3,2,1,0:T(1,128)S(1)}, f32[6,2,1,128]{3,2,1,0:T(1,128)S(1)}, u32[]{:S(2)}, u32[]{:S(2)}) collective-permute-start(f32[6,2,1,128]{3,2,1,0:T(1,128)S(1)} %get-tuple-element.303), channel_id=1, source_target_pairs={{4,0},{8,4},{12,8},{5,1},{9,5},{13,9},{6,2},{10,6},{14,10},{7,3},{... | collective-permute-start | bytes 18440 | tf_op jit(solution)/shard_map/ppermute | solution.py:31
  211.6 8.8 %collective-permute-start.54 = (f32[6,2,1,128]{3,2,1,0:T(1,128)S(1)}, f32[6,2,1,128]{3,2,1,0:T(1,128)S(1)}, u32[]{:S(2)}, u32[]{:S(2)}) collective-permute-start(f32[6,2,1,128]{3,2,1,0:T(1,128)S(1)} %get-tuple-element.302), channel_id=1, source_target_pairs={{0,4},{4,8},{8,12},{1,5},{5,9},{9,13},{2,6},{6,10},{10,14},{3,7},{... | collective-permute-start | bytes 18440 | tf_op jit(solution)/shard_map/ppermute | solution.py:29
  221.1 8.0 %collective-permute-start.57 = (f32[6,2,18,1]{3,2,1,0:T(8,128)S(1)}, f32[6,2,18,1]{3,2,1,0:T(8,128)S(1)}, u32[]{:S(2)}, u32[]{:S(2)}) collective-permute-start(f32[6,2,18,1]{3,2,1,0:T(8,128)S(1)} %get-tuple-element.261), channel_id=1, source_target_pairs={{2,0},{3,1},{6,4},{7,5},{10,8},{11,9},{14,12},{15,13},{18,16},{19,... | collective-permute-start | bytes 2600 | tf_op jit(solution)/shard_map/ppermute | solution.py:31
  222.4 7.9 %collective-permute-start.56 = (f32[6,2,18,1]{3,2,1,0:T(8,128)S(1)}, f32[6,2,18,1]{3,2,1,0:T(8,128)S(1)}, u32[]{:S(2)}, u32[]{:S(2)}) collective-permute-start(f32[6,2,18,1]{3,2,1,0:T(8,128)S(1)} %get-tuple-element.260), channel_id=1, source_target_pairs={{0,2},{1,3},{4,6},{5,7},{8,10},{9,11},{12,14},{13,15},{16,18},{17,... | collective-permute-start | bytes 2600 | tf_op jit(solution)/shard_map/ppermute | solution.py:29
  230.6 7.8 %collective-permute-start.59 = (f32[6,1,18,130]{3,2,1,0:T(8,128)S(1)}, f32[6,1,18,130]{3,2,1,0:T(8,128)S(1)}, u32[]{:S(2)}, u32[]{:S(2)}) collective-permute-start(f32[6,1,18,130]{3,2,1,0:T(8,128)S(1)} %get-tuple-element.223), channel_id=1, source_target_pairs={{1,0},{3,2},{5,4},{7,6},{9,8},{11,10},{13,12},{15,14},{17,16},{19,... | collective-permute-start | bytes 168488 | tf_op jit(solution)/shard_map/ppermute | solution.py:31
  (91 other events, 502.0 us)
where the time goes:
time: 397 us; the launch traced here: 392 us
  starting transfers between devices  289 us (73%)
  waiting for transfers between devices  60.2 us (15%)
  other arithmetic  17.4 us (4%)
  blocking collectives  14.2 us (4%)
  local copies, waits for them, and re-layouts  7.28 us (2%)
    ppermute x54, starting transfers between devices, with_halo(): lax.ppermute(tail, axis, [(i, (i + 1) % count) for i in range(ends)])  219 us
    ppermute x54, starting transfers between devices, with_halo(): lax.ppermute(head, axis, [((i + 1) % count, i) for i in range(ends)])  69.9 us
    ppermute x54, waiting for transfers between devices, with_halo(): lax.ppermute(tail, axis, [(i, (i + 1) % count) for i in range(ends)])  49.1 us
    ppermute x54, waiting for transfers between devices, with_halo(): lax.ppermute(head, axis, [((i + 1) % count, i) for i in range(ends)])  11.1 us
  transfers between devices with their start and end apart: 108, of which 56 were waited for; matrix products, arithmetic and copies ran while one was open for 2% of the time, Pallas kernels for 0%

commit v1 on v0

v1 whole, which is shorter than its diff:
```python
import functools

import jax
import jax.numpy as jnp
from jax import lax
from jax.experimental import pallas as pl
from jax.experimental.pallas import tpu as pltpu
from jax.sharding import PartitionSpec as P

SUBSTEPS = 4
LLG_STEPS = 2
REACH = 2 * SUBSTEPS * LLG_STEPS
PAD = 8
ELASTIC_STEP = 0.3
SPIN_STEP = 0.04
DAMPING = 0.3
FORCE_SCALE = 0.25
SPONGE_RATE = 0.08
POISSON = 0.2
MESH = pl.DeviceIdType.MESH


def kernel(
    sizes,
    wave, buoy, sponge, spin, regions, table,
    wave_out, spin_out,
    W, B, G, A, F, M, MAT, K, FORCE, PKS, PKR, MOWN, WX, FX,
    xs_sem, xr_sem, ps_sem, pr_sem, fs_sem, fr_sem, ys_sem, yr_sem, os_sem, or_sem, l_sem,
):
    n_x, n_y = sizes
    g = lax.axis_index("groups")
    x = lax.axis_index("gx")
    y = lax.axis_index("gy")
    h = lax.axis_index("gz")
    rows = wave.shape[2]
    halo = REACH
    depth = wave.shape[1]
    layers = spin.shape[1]
    lo0, own0, hi0 = PAD, PAD + halo, PAD + halo + rows
    total = rows + 2 * halo
    span = slice(PAD, PAD + total)
    own = slice(own0, own0 + rows)

    partner = (g, x, y, 1 - h)
    has_lo, has_hi = x > 0, x < n_x - 1
    has_left, has_right = y > 0, y < n_y - 1
    step_y = 1 - 2 * h
    y_to = y + step_y
    y_from = y - step_y
    sends_y = jnp.logical_and(y_to >= 0, y_to < n_y)
    takes_y = jnp.logical_and(y_from >= 0, y_from < n_y)

    barrier = pltpu.get_barrier_semaphore()

    def greet(cond, dev):
        @pl.when(cond)
        def _():
            pl.semaphore_signal(barrier, inc=1, device_id=dev, device_id_type=MESH)

    pl.semaphore_signal(barrier, inc=1, device_id=partner, device_id_type=MESH)
    greet(has_lo, (g, x - 1, y, h))
    greet(has_hi, (g, x + 1, y, h))
    greet(has_left, (g, x, y - 1, h))
    greet(has_right, (g, x, y + 1, h))

    lane_own = lax.broadcasted_iota(jnp.int32, (rows, 128), 1)
    region = jnp.broadcast_to(regions[...], (rows, 128))
    packed = jnp.zeros((rows, 128), jnp.float32)
    for p in range(4):
        value = jnp.zeros((rows, 128), jnp.float32)
        for r in range(table.shape[1]):
            value = jnp.where(region == r, table[p, r], value)
        packed = jnp.where(lane_own // 32 == p, value, packed)
    MOWN[...] = packed

    i32 = lambda c: jnp.where(c, 1, 0).astype(jnp.int32)
    pl.semaphore_wait(barrier, 1 + i32(has_lo) + i32(has_hi) + i32(has_left) + i32(has_right))

    d0 = 1 + depth * h
    b0 = depth * h
    f0 = layers * h

    def piece(i, r):
        rr = pl.ds(r, rows)
        return [
            (spin, F.at[0, :, pl.ds(f0, layers), rr]),
            (MOWN, M.at[rr]),
            (wave.at[3:9, 0:1], W.at[3:9, pl.ds(d0, 1), rr]),
            (wave.at[0:3], W.at[0:3, pl.ds(d0, depth), rr]),
            (wave.at[3:9, 1:depth], W.at[3:9, pl.ds(d0 + 1, depth - 1), rr]),
            (buoy, B.at[pl.ds(b0, depth), rr]),
            (sponge, G.at[pl.ds(b0, depth), rr]),
        ][i]

    count = 7
    with_partner = (0, 2, 3, 4, 5, 6)
    group_a, group_b = (0, 1, 2), (3, 4, 5, 6)

    def x_copy(i, up):
        src, dst = piece(i, lo0 if up else hi0)
        return pltpu.make_async_remote_copy(
            src_ref=src, dst_ref=dst, send_sem=xs_sem.at[i, 0 if up else 1],
            recv_sem=xr_sem.at[i, 0 if up else 1],
            device_id=(g, x + 1 if up else x - 1, y, h), device_id_type=MESH)

    def own_copy(i):
        src, dst = piece(i, own0)
        return pltpu.make_async_remote_copy(
            src_ref=src, dst_ref=dst, send_sem=ps_sem.at[i], recv_sem=pr_sem.at[i],
            device_id=partner, device_id_type=MESH)

    def forward(i, low):
        _, dst = piece(i, lo0 if low else hi0)
        k = 0 if low else 1
        return pltpu.make_async_remote_copy(
            src_ref=dst, dst_ref=dst, send_sem=fs_sem.at[i, k], recv_sem=fr_sem.at[i, k],
            device_id=partner, device_id_type=MESH)

    def local_copy(i):
        src, dst = piece(i, own0)
        return pltpu.make_async_copy(src, dst, l_sem.at[i])

    for i in range(count):
        @pl.when(has_hi)
        def _():
            x_copy(i, True).start()

        @pl.when(has_lo)
        def _():
            x_copy(i, False).start()

    for i in range(count):
        if i in with_partner:
            own_copy(i).start()
        local_copy(i).start()

    zero_row = jnp.zeros((PAD, 128), jnp.float32)

    for c in range(9):
        for d in (0, 1 + 2 * depth):
            W[c, d] = jnp.zeros((total + 2 * PAD, 128), jnp.float32)

    def pad_rows(d, carry):
        for c in range(9):
            W[c, d, 0:PAD] = zero_row
            W[c, d, PAD + total:] = zero_row
        return carry

    lax.fori_loop(1, 1 + 2 * depth, pad_rows, 0)

    def pad_film(l, carry):
        for c in range(3):
            for b in range(2):
                F[b, c, l, 0:PAD] = zero_row
                F[b, c, l, PAD + total:] = zero_row
        return carry

    lax.fori_loop(0, 2 * layers, pad_film, 0)
    for c in range(3):
        for d in range(1, 2 * depth):
            FORCE[d, c] = jnp.zeros((total, 128), jnp.float32)

    @pl.when(jnp.logical_not(takes_y))
    def _():
        PKR[...] = jnp.zeros_like(PKR)

    lane = lax.broadcasted_iota(jnp.int32, (total, 128), 1)
    row = lax.broadcasted_iota(jnp.int32, (total, 128), 0)
    slot = lax.rem(lane // 16 + (1 - h), 8)
    halo_lane = slot == 0
    halo_film = jnp.logical_and(halo_lane, takes_y)

    def arrive(group):
        for i in group:
            @pl.when(has_lo)
            def _():
                x_copy(i, True).wait_recv()
                if i in with_partner:
                    forward(i, True).start()

            @pl.when(has_hi)
            def _():
                x_copy(i, False).wait_recv()
                if i in with_partner:
                    forward(i, False).start()

        for i in group:
            local_copy(i).wait()
            if i in with_partner:
                own_copy(i).wait_recv()

                @pl.when(has_lo)
                def _():
                    forward(i, True).wait_recv()

                @pl.when(has_hi)
                def _():
                    forward(i, False).wait_recv()

    def sent(group):
        for i in group:
            if i in with_partner:
                own_copy(i).wait_send()

            @pl.when(has_hi)
            def _():
                x_copy(i, True).wait_send()
                if i in with_partner:
                    forward(i, False).wait_send()

            @pl.when(has_lo)
            def _():
                x_copy(i, False).wait_send()
                if i in with_partner:
                    forward(i, True).wait_send()

    def fill(refs, cond, r, zero):
        rr = slice(r, r + rows)

        @pl.when(jnp.logical_not(cond))
        def _():
            for ref in refs:
                ref[..., rr, :] = jnp.zeros_like(ref[..., rr, :]) if zero else ref[..., own, :]

    def pack(planes, first):
        for k in range(0, len(planes), 8):
            out = jnp.zeros((total, 128), jnp.float32)
            for j, ref in enumerate(planes[k:k + 8]):
                value = ref[span]
                if j:
                    value = pltpu.roll(value, 16 * j, 1)
                out = jnp.where(slot == j, value, out)
            PKS[first + k // 8] = out

    def unpack(planes, first, mask):
        for k in range(0, len(planes), 8):
            got = PKR[first + k // 8]
            for j, ref in enumerate(planes[k:k + 8]):
                value = pltpu.roll(got, 128 - 16 * j, 1) if j else got
                ref[span] = jnp.where(mask, value, ref[span])

    film_planes = [F.at[0, c, l] for c in range(3) for l in range(2 * layers)]
    stress = range(3, 9)
    first_stress = [W.at[c, 1] for c in stress] + [W.at[c, 1 + depth] for c in stress]
    rest = [W.at[c, 1 + d] for c in range(3) for d in range(2 * depth)]
    rest += [W.at[c, 1 + d] for c in stress for d in range(2 * depth) if d % depth]
    coefs = [B.at[d] for d in range(2 * depth)] + [A.at[d] for d in range(2 * depth)]
    early, late = first_stress[:8], first_stress[8:] + rest + coefs
    n_film = len(film_planes) // 8
    n_a = n_film + 2
    n_b = (len(late) + 7) // 8

    def y_copy(k):
        sl = pl.ds(0, n_a) if k == 0 else pl.ds(n_a, n_b)
        return pltpu.make_async_remote_copy(
            src_ref=PKS.at[sl], dst_ref=PKR.at[sl], send_sem=ys_sem.at[k], recv_sem=yr_sem.at[k],
            device_id=(g, x, y_to, h), device_id_type=MESH)

    def y_start(k):
        @pl.when(sends_y)
        def _():
            y_copy(k).start()

    def y_wait(k):
        @pl.when(sends_y)
        def _():
            y_copy(k).wait_send()

        @pl.when(takes_y)
        def _():
            y_copy(k).wait_recv()

    arrive(group_a)
    for cond, r in ((has_lo, lo0), (has_hi, hi0)):
        fill([F.at[0], M], cond, r, False)
        fill([W.at[3:9, 1:2], W.at[3:9, 1 + depth:2 + depth]], cond, r, True)
    pack(film_planes, 0)
    pack(early, n_film)
    PKS[n_film + 1] = M[span]
    y_start(0)

    arrive(group_b)
    for cond, r in ((has_lo, lo0), (has_hi, hi0)):
        fill([B], cond, r, False)
        fill([W.at[0:3, 1:1 + 2 * depth]], cond, r, True)
        for d in range(2 * depth):
            if d % depth:
                fill([W.at[3:9, 1 + d:2 + d]], cond, r, True)
    inside = jnp.logical_and(
        jnp.logical_or(row >= halo, has_lo), jnp.logical_or(row < halo + rows, has_hi))
    for d in range(2 * depth):
        A[d, span] = jnp.where(inside, 1.0 - SPONGE_RATE * G[d, span].astype(jnp.float32), 0.0)
    pack(late, n_a)
    y_start(1)

    sent(group_a)
    y_wait(0)
    unpack(film_planes, 0, halo_film)
    unpack(early, n_film, halo_lane)
    mine, other = M[span], PKR[n_film + 1]
    for p in range(4):
        at = slice(32 * p, 32 * p + 1)
        MAT[p] = jnp.where(
            halo_film, jnp.broadcast_to(other[:, at], (total, 128)),
            jnp.broadcast_to(mine[:, at], (total, 128)))

    def spin_step(now, r0, n):
        new = 1 - now
        rr, mm = slice(PAD + r0, PAD + r0 + n), slice(r0, r0 + n)
        s = [W[c, 1, rr] for c in stress]
        an, nc, sc = MAT[0, mm], MAT[2, mm], MAT[3, mm]
        part = POISSON * (s[0] + s[1] + s[2])
        K[0, mm] = -6.0 - nc * (s[0] - part)
        K[1, mm] = -6.0 - nc * (s[1] - part)
        K[2, mm] = -6.0 - nc * (s[2] - part) + 2.0 * an
        for q in (3, 4, 5):
            K[q, mm] = -(sc * s[q])
        lanes = lax.broadcasted_iota(jnp.int32, (n, 128), 1)
        at_rows = lax.broadcasted_iota(jnp.int32, (n, 128), 0) + r0
        x_first = jnp.logical_and(at_rows == halo, x == 0)
        x_last = jnp.logical_and(at_rows == halo + rows - 1, x == n_x - 1)
        y_first = jnp.logical_and(lanes == 0, jnp.logical_and(y == 0, h == 0))
        y_last = jnp.logical_and(lanes == 127, jnp.logical_and(y == n_y - 1, h == 1))
        factor = SPIN_STEP / (1.0 + DAMPING * DAMPING)

        def layer(l, sums):
            up, down = jnp.minimum(l + 1, 2 * layers - 1), jnp.maximum(l - 1, 0)
            m, lap, dx, dy = [], [], [], []
            for c in range(3):
                mid = F[now, c, l, rr]
                xp = jnp.where(x_last, mid, F[now, c, l, PAD + r0 + 1:PAD + r0 + 1 + n])
                xm = jnp.where(x_first, mid, F[now, c, l, PAD + r0 - 1:PAD + r0 - 1 + n])
                yp = jnp.where(y_last, mid, pltpu.roll(mid, 127, 1))
                ym = jnp.where(y_first, mid, pltpu.roll(mid, 1, 1))
                m.append(mid)
                lap.append(F[now, c, up, rr] + F[now, c, down, rr] + xp + xm + yp + ym)
                dx.append(xp - xm if c != 1 else None)
                dy.append(yp - ym if c != 0 else None)
            mx, my, mz = m
            half = 0.5 * MAT[1, mm]
            hx = lap[0] + half * dx[2] + K[0, mm] * mx + K[5, mm] * my + K[4, mm] * mz
            hy = lap[1] + half * dy[2] + K[5, mm] * mx + K[1, mm] * my + K[3, mm] * mz
            hz = lap[2] - half * (dx[0] + dy[1]) + K[4, mm] * mx + K[3, mm] * my + K[2, mm] * mz
            tx = my * hz - mz * hy
            ty = mz * hx - mx * hz
            tz = mx * hy - my * hx
            qx = mx - factor * (tx + DAMPING * (my * tz - mz * ty))
            qy = my - factor * (ty + DAMPING * (mz * tx - mx * tz))
            qz = mz - factor * (tz + DAMPING * (mx * ty - my * tx))
            square = qx * qx + qy * qy + qz * qz
            inv = lax.rsqrt(square)
            inv = inv * (1.5 - 0.5 * square * inv * inv)
            qx, qy, qz = qx * inv, qy * inv, qz * inv
            F[new, 0, l, rr] = qx
            F[new, 1, l, rr] = qy
            F[new, 2, l, rr] = qz
            return sums[0] + qx * qz, sums[1] + qy * qz, sums[2] + (qz * qz - 1.0 / 3.0)

        zero = jnp.zeros((n, 128), jnp.float32)
        sums = lax.fori_loop(0, 2 * layers, layer, (zero, zero, zero))
        sc, nc = MAT[3, mm], MAT[2, mm]
        FORCE[0, 0, mm] = (2.0 * FORCE_SCALE) * (sc * sums[0])
        FORCE[0, 1, mm] = (2.0 * FORCE_SCALE) * (sc * sums[1])
        FORCE[0, 2, mm] = (2.0 * FORCE_SCALE) * (nc * sums[2])

    def elastic(r0, n):
        lo = PAD + r0
        rr, mm = slice(lo, lo + n), slice(r0, r0 + n)

        def dx(c, d):
            return W[c, d, lo + 1:lo + 1 + n] - W[c, d, lo - 1:lo - 1 + n]

        def dy(c, d):
            value = W[c, d, rr]
            return pltpu.roll(value, 127, 1) - pltpu.roll(value, 1, 1)

        def dz(c, d):
            return W[c, d + 1, rr] - W[c, d - 1, rr]

        def velocity(k, carry):
            d = k + 1
            a, b = A[k, rr], B[k, rr]
            W[0, d, rr] = a * W[0, d, rr] + b * (dx(3, d) + dy(8, d) + dz(7, d) + FORCE[k, 0, mm])
            W[1, d, rr] = a * W[1, d, rr] + b * (dx(8, d) + dy(4, d) + dz(6, d) + FORCE[k, 1, mm])
            W[2, d, rr] = a * W[2, d, rr] + b * (dx(7, d) + dy(6, d) + dz(5, d) + FORCE[k, 2, mm])
            return carry

        def stresses(k, carry):
            d = k + 1
            a = A[k, rr]
            b = (0.5 * ELASTIC_STEP) * a
            xx, yy, zz = dx(0, d), dy(1, d), dz(2, d)
            trace = xx + yy + zz
            W[3, d, rr] = a * W[3, d, rr] + b * (trace + 2.0 * xx)
            W[4, d, rr] = a * W[4, d, rr] + b * (trace + 2.0 * yy)
            W[5, d, rr] = a * W[5, d, rr] + b * (trace + 2.0 * zz)
            W[6, d, rr] = a * W[6, d, rr] + b * (dz(1, d) + dy(2, d))
            W[7, d, rr] = a * W[7, d, rr] + b * (dz(0, d) + dx(2, d))
            W[8, d, rr] = a * W[8, d, rr] + b * (dy(0, d) + dx(1, d))
            return carry

        def substep(_, carry):
            lax.fori_loop(0, 2 * depth, velocity, 0)
            lax.fori_loop(0, 2 * depth, stresses, 0)
            return carry

        lax.fori_loop(0, SUBSTEPS, substep, 0)

    spin_step(0, 0, total)

    sent(group_b)
    y_wait(1)
    unpack(late, n_a, halo_lane)
    for d in range(2 * depth):
        B[d, span] = (0.5 * ELASTIC_STEP) * A[d, span] * B[d, span]

    elastic(0, total)
    spin_step(1, 2 * SUBSTEPS, total - 4 * SUBSTEPS)

    far_f = pl.ds(layers * (1 - h), layers)
    far_d = pl.ds(1 + depth * (1 - h), depth)
    film_swap = pltpu.make_async_remote_copy(
        src_ref=F.at[0, :, far_f, pl.ds(own0, rows)], dst_ref=FX, send_sem=os_sem.at[0],
        recv_sem=or_sem.at[0], device_id=partner, device_id_type=MESH)
    film_swap.start()
    elastic(2 * SUBSTEPS, total - 4 * SUBSTEPS)
    wave_swap = pltpu.make_async_remote_copy(
        src_ref=W.at[:, far_d, pl.ds(own0, rows)], dst_ref=WX, send_sem=os_sem.at[1],
        recv_sem=or_sem.at[1], device_id=partner, device_id_type=MESH)
    wave_swap.start()

    mine = lane_own // 64 == h
    film_swap.wait()
    for c in range(3):
        for l in range(layers):
            spin_out[c, l] = jnp.where(mine, F[0, c, f0 + l, own], FX[c, l])
    wave_swap.wait()
    for c in range(9):
        for d in range(depth):
            wave_out[c, d] = jnp.where(mine, W[c, d0 + d, own], WX[c, d])


def body(sizes, wave, buoy, sponge, spin, regions, table):
    depth, rows, lanes = wave.shape[1:]
    layers = spin.shape[1]
    total = rows + 2 * REACH
    tall = total + 2 * PAD
    f32 = lambda *s: pltpu.VMEM(s, jnp.float32)
    dma = lambda *s: pltpu.SemaphoreType.DMA(s)
    n_pk = 3 * 2 * layers // 8 + 2 + (11 * 2 * depth - 8 + 7) // 8
    vmem = pl.BlockSpec(memory_space=pltpu.VMEM)
    return pl.pallas_call(
        functools.partial(kernel, sizes),
        name="film_and_substrate",
        out_shape=(
            jax.ShapeDtypeStruct(wave.shape, jnp.float32),
            jax.ShapeDtypeStruct(spin.shape, jnp.float32),
        ),
        in_specs=[vmem] * 5 + [pl.BlockSpec(memory_space=pltpu.SMEM)],
        out_specs=(vmem, vmem),
        scratch_shapes=[
            f32(9, 2 * depth + 2, tall, lanes),
            f32(2 * depth, tall, lanes),
            pltpu.VMEM((2 * depth, tall, lanes), jnp.int32),
            f32(2 * depth, tall, lanes),
            f32(2, 3, 2 * layers, tall, lanes),
            f32(tall, lanes),
            f32(4, total, lanes),
            f32(6, total, lanes),
            f32(2 * depth, 3, total, lanes),
            f32(n_pk, total, lanes),
            f32(n_pk, total, lanes),
            f32(rows, lanes),
            f32(9, depth, rows, lanes),
            f32(3, layers, rows, lanes),
            dma(7, 2), dma(7, 2), dma(7), dma(7), dma(7, 2), dma(7, 2),
            dma(2), dma(2), dma(2), dma(2), dma(7),
        ],
        compiler_params=pltpu.CompilerParams(
            collective_id=0, has_side_effects=True, vmem_limit_bytes=40 * 2**20),
    )(wave, buoy, sponge, spin, regions, table)


def solution(mesh):
    sizes = (mesh.shape["gx"], mesh.shape["gy"])
    return jax.shard_map(
        functools.partial(body, sizes),
        mesh=mesh,
        in_specs=(
            P("groups", "gz", "gx", "gy"),
            P(("groups", "gz"), "gx", "gy"),
            P(("groups", "gz"), "gx", "gy"),
            P("groups", "gz", "gx", "gy"),
            P(("groups", "gx"), "gy"),
            P(),
        ),
        out_specs=(P("groups", "gz", "gx", "gy"), P("groups", "gz", "gx", "gy")),
        check_vma=False,
    )
```

time: 397 us -> 32.7 us (0.08); the launches traced: 392 us -> 32.4 us
  starting transfers between devices: 289 us -> 0 us
  waiting for transfers between devices: 60.2 us -> 0 us
  Pallas kernels: 0 us -> 26.4 us
  other arithmetic: 17.4 us -> 0 us
  blocking collectives: 14.2 us -> 0 us
    ppermute x108 -> x0, starting transfers between devices: 289 us -> none  [the longest x54 219 us: with_halo(): lax.ppermute(tail, axis, [(i, (i + 1) % count) for i in range(ends)])]
    ppermute x108 -> x0, waiting for transfers between devices: 60.2 us -> none  [the longest x54 49.1 us: with_halo(): lax.ppermute(tail, axis, [(i, (i + 1) % count) for i in range(ends)])]
    pallas_call x0 -> x1, Pallas kernels: none -> 26.4 us  [body(): pl.pallas_call(functools.partial(kernel, sizes), name='film_and_substrate...]
    psum x4 -> x0, blocking collectives: 14.2 us -> none  [the longest x2 7.18 us: from_root(): return lax.psum(jnp.where(mine, array, jnp.zeros_like(array)), axis)]
    concatenate x55 -> x0, other arithmetic: 7.83 us -> none  [the longest x50 6.53 us: with_halo(): jnp.concatenate([lax.ppermute(tail, axis, [(i, (i + 1) % count) for i in...]
    slice x57 -> x0, local copies, waits for them, and re-layouts: 3.97 us -> none  [the longest x52 3.68 us: with_halo(): lax.slice_in_dim(cells, cells.shape[dim] - width, cells.shape[dim], axis=...]
  transfers between devices with their start and end apart: 108 -> 0, of which waited for: 56 -> 0; matrix products, arithmetic and copies ran while one was open for 2% -> 0% of each run, Pallas kernels for 0% -> 0%
where the time goes in v1:
time: 32.7 us; the launch traced here: 32.4 us
  Pallas kernels  26.4 us (81%)
  local copies, waits for them, and re-layouts  5.28 us (16%)
  between operations  0.65 us (2%)
    pallas_call x1, Pallas kernels, body(): pl.pallas_call(functools.partial(kernel, sizes), name='film_and_substrate...  26.4 us
    unnamed x13, local copies, waits for them, and re-layouts  5.28 us

profile of v1, /device:TPU:0, one launch (start us, length us, event | category | flops | bytes accessed | tf_op | source)
XLA Modules:
  0.0 32.4 jit_solution(18202196713633209961)
XLA Ops:
  0.6 0.0 copy-start.4
  0.6 0.7 %copy.8.regions = s32[16,1]{1,0:T(8,128)S(1)} copy(s32[16,1]{0,1:T(1,128)} %param.10) | data formatting | bytes 128 | tf_op args[4]
  1.4 0.0 copy-done.4
  1.4 0.0 copy-start
  1.4 0.9 %copy-done = f32[9,2,16,128]{3,2,1,0:T(8,128)S(1)} copy-done((f32[9,2,16,128]{3,2,1,0:T(8,128)S(1)}, f32[9,2,16,128]{3,2,1,0:T(8,128)}, u32[]{:S(2)}) %copy-start) | copy-done | bytes 147480
  2.3 0.0 copy-start.1
  2.3 0.9 %copy-done.1 = f32[3,4,16,128]{3,2,1,0:T(8,128)S(1)} copy-done((f32[3,4,16,128]{3,2,1,0:T(8,128)S(1)}, f32[3,4,16,128]{3,2,1,0:T(8,128)}, u32[]{:S(2)}) %copy-start.1) | copy-done | bytes 98328
  3.2 0.0 copy-start.2
  3.2 0.7 %copy-done.2 = f32[2,16,128]{2,1,0:T(8,128)S(1)} copy-done((f32[2,16,128]{2,1,0:T(8,128)S(1)}, f32[2,16,128]{2,1,0:T(8,128)}, u32[]{:S(2)}) %copy-start.2) | copy-done | bytes 16408
  3.9 0.0 copy-start.3
  3.9 0.7 %copy-done.3 = s32[2,16,128]{2,1,0:T(8,128)S(1)} copy-done((s32[2,16,128]{2,1,0:T(8,128)S(1)}, s32[2,16,128]{2,1,0:T(8,128)}, u32[]{:S(2)}) %copy-start.3) | copy-done | bytes 16408
  4.6 26.4 %film_and_substrate.1 = (f32[9,2,16,128]{3,2,1,0:T(8,128)S(1)}, f32[3,4,16,128]{3,2,1,0:T(8,128)S(1)}) custom-call(f32[9,2,16,128]{3,2,1,0:T(8,128)S(1)} %copy-done, f32[2,16,128]{2,1,0:T(8,128)S(1)} %copy-done.2, s32[2,16,128]{2,1,0:T(8,128)S(1)} %copy-done.3, f32[3,4,16,128]{3,2,1,0:T(8,128)S(1)} %copy-done.1, s32[16,1]{1,0:T(8,128)S(1)} %copy.8.regions, ...), custom_call_target="tpu_custom_call" | custom-call | tf_op jit(solution)/shard_map/film_and_substrate/pallas_call | solution.py:452
  31.1 0.7 %copy.11 = f32[9,2,16,128]{3,2,1,0:T(8,128)} copy(f32[9,2,16,128]{3,2,1,0:T(8,128)S(1)} %get-tuple-element.4) | data formatting | bytes 294912
  31.7 0.6 %copy.12 = f32[3,4,16,128]{3,2,1,0:T(8,128)} copy(f32[3,4,16,128]{3,2,1,0:T(8,128)S(1)} %get-tuple-element.5) | data formatting | bytes 196608
Async XLA Ops:
  0.6 0.8 %copy-start.4 = (f32[4,4]{1,0:T(4,128)S(1)}, f32[4,4]{1,0:T(4,128)}, u32[]{:S(2)}) copy-start(f32[4,4]{1,0:T(4,128)} %table.1) | copy-start | bytes 196
  1.4 0.9 %copy-start = (f32[9,2,16,128]{3,2,1,0:T(8,128)S(1)}, f32[9,2,16,128]{3,2,1,0:T(8,128)}, u32[]{:S(2)}) copy-start(f32[9,2,16,128]{3,2,1,0:T(8,128)} %wave.1) | copy-start | bytes 442372
  2.3 0.9 %copy-start.1 = (f32[3,4,16,128]{3,2,1,0:T(8,128)S(1)}, f32[3,4,16,128]{3,2,1,0:T(8,128)}, u32[]{:S(2)}) copy-start(f32[3,4,16,128]{3,2,1,0:T(8,128)} %spin.1) | copy-start | bytes 294916
  3.2 0.7 %copy-start.2 = (f32[2,16,128]{2,1,0:T(8,128)S(1)}, f32[2,16,128]{2,1,0:T(8,128)}, u32[]{:S(2)}) copy-start(f32[2,16,128]{2,1,0:T(8,128)} %buoy.1) | copy-start | bytes 49156
  3.9 0.7 %copy-start.3 = (s32[2,16,128]{2,1,0:T(8,128)S(1)}, s32[2,16,128]{2,1,0:T(8,128)}, u32[]{:S(2)}) copy-start(s32[2,16,128]{2,1,0:T(8,128)} %sponge.1) | copy-start | bytes 49156

commit v2 on v1

--- a/solution.py
+++ b/solution.py
@@ -156,10 +156,6 @@
         return carry
 
     lax.fori_loop(0, 2 * layers, pad_film, 0)
-    for c in range(3):
-        for d in range(1, 2 * depth):
-            FORCE[d, c] = jnp.zeros((total, 128), jnp.float32)
-
     @pl.when(jnp.logical_not(takes_y))
     def _():
         PKR[...] = jnp.zeros_like(PKR)
@@ -324,7 +320,7 @@
         factor = SPIN_STEP / (1.0 + DAMPING * DAMPING)
 
         def layer(l, sums):
-            up, down = jnp.minimum(l + 1, 2 * layers - 1), jnp.maximum(l - 1, 0)
+            up, down = min(l + 1, 2 * layers - 1), max(l - 1, 0)
             m, lap, dx, dy = [], [], [], []
             for c in range(3):
                 mid = F[now, c, l, rr]
@@ -357,11 +353,13 @@
             return sums[0] + qx * qz, sums[1] + qy * qz, sums[2] + (qz * qz - 1.0 / 3.0)
 
         zero = jnp.zeros((n, 128), jnp.float32)
-        sums = lax.fori_loop(0, 2 * layers, layer, (zero, zero, zero))
+        sums = (zero, zero, zero)
+        for l in range(2 * layers):
+            sums = layer(l, sums)
         sc, nc = MAT[3, mm], MAT[2, mm]
-        FORCE[0, 0, mm] = (2.0 * FORCE_SCALE) * (sc * sums[0])
-        FORCE[0, 1, mm] = (2.0 * FORCE_SCALE) * (sc * sums[1])
-        FORCE[0, 2, mm] = (2.0 * FORCE_SCALE) * (nc * sums[2])
+        FORCE[0, mm] = (2.0 * FORCE_SCALE) * (sc * sums[0])
+        FORCE[1, mm] = (2.0 * FORCE_SCALE) * (sc * sums[1])
+        FORCE[2, mm] = (2.0 * FORCE_SCALE) * (nc * sums[2])
 
     def elastic(r0, n):
         lo = PAD + r0
@@ -377,12 +375,15 @@
         def dz(c, d):
             return W[c, d + 1, rr] - W[c, d - 1, rr]
 
+        def push(k, c):
+            return FORCE[c, mm] if k == 0 else 0.0
+
         def velocity(k, carry):
             d = k + 1
             a, b = A[k, rr], B[k, rr]
-            W[0, d, rr] = a * W[0, d, rr] + b * (dx(3, d) + dy(8, d) + dz(7, d) + FORCE[k, 0, mm])
-            W[1, d, rr] = a * W[1, d, rr] + b * (dx(8, d) + dy(4, d) + dz(6, d) + FORCE[k, 1, mm])
-            W[2, d, rr] = a * W[2, d, rr] + b * (dx(7, d) + dy(6, d) + dz(5, d) + FORCE[k, 2, mm])
+            W[0, d, rr] = a * W[0, d, rr] + b * (dx(3, d) + dy(8, d) + dz(7, d) + push(k, 0))
+            W[1, d, rr] = a * W[1, d, rr] + b * (dx(8, d) + dy(4, d) + dz(6, d) + push(k, 1))
+            W[2, d, rr] = a * W[2, d, rr] + b * (dx(7, d) + dy(6, d) + dz(5, d) + push(k, 2))
             return carry
 
         def stresses(k, carry):
@@ -400,8 +401,10 @@
             return carry
 
         def substep(_, carry):
-            lax.fori_loop(0, 2 * depth, velocity, 0)
-            lax.fori_loop(0, 2 * depth, stresses, 0)
+            for k in range(2 * depth):
+                velocity(k, 0)
+            for k in range(2 * depth):
+                stresses(k, 0)
             return carry
 
         lax.fori_loop(0, SUBSTEPS, substep, 0)
@@ -467,7 +470,7 @@
             f32(tall, lanes),
             f32(4, total, lanes),
             f32(6, total, lanes),
-            f32(2 * depth, 3, total, lanes),
+            f32(3, total, lanes),
             f32(n_pk, total, lanes),
             f32(n_pk, total, lanes),
             f32(rows, lanes),

time: 32.7 us -> 28.1 us (0.86)
  Pallas kernels: 26.4 us -> 21.8 us
    pallas_call x1, Pallas kernels: 26.4 us -> 21.8 us  [body(): pl.pallas_call(functools.partial(kernel, sizes), name='film_and_substrate...]
where the time goes in v2:
time: 28.1 us; the launch traced here: 27.7 us
  Pallas kernels  21.8 us (78%)
  local copies, waits for them, and re-layouts  5.28 us (19%)
  between operations  0.65 us (2%)
    pallas_call x1, Pallas kernels, body(): pl.pallas_call(functools.partial(kernel, sizes), name='film_and_substrate...  21.8 us
    unnamed x13, local copies, waits for them, and re-layouts  5.28 us

profile of v2, /device:TPU:0, one launch (start us, length us, event | category | flops | bytes accessed | tf_op | source)
XLA Modules:
  0.0 27.7 jit_solution(18387645038896479368)
XLA Ops:
  0.6 0.0 copy-start.4
  0.6 0.7 %copy.8.regions = s32[16,1]{1,0:T(8,128)S(1)} copy(s32[16,1]{0,1:T(1,128)} %param.10) | data formatting | bytes 128 | tf_op args[4]
  1.4 0.0 copy-done.4
  1.4 0.0 copy-start
  1.4 0.9 %copy-done = f32[9,2,16,128]{3,2,1,0:T(8,128)S(1)} copy-done((f32[9,2,16,128]{3,2,1,0:T(8,128)S(1)}, f32[9,2,16,128]{3,2,1,0:T(8,128)}, u32[]{:S(2)}) %copy-start) | copy-done | bytes 147480
  2.3 0.0 copy-start.1
  2.3 0.9 %copy-done.1 = f32[3,4,16,128]{3,2,1,0:T(8,128)S(1)} copy-done((f32[3,4,16,128]{3,2,1,0:T(8,128)S(1)}, f32[3,4,16,128]{3,2,1,0:T(8,128)}, u32[]{:S(2)}) %copy-start.1) | copy-done | bytes 98328
  3.2 0.0 copy-start.2
  3.2 0.7 %copy-done.2 = f32[2,16,128]{2,1,0:T(8,128)S(1)} copy-done((f32[2,16,128]{2,1,0:T(8,128)S(1)}, f32[2,16,128]{2,1,0:T(8,128)}, u32[]{:S(2)}) %copy-start.2) | copy-done | bytes 16408
  3.9 0.0 copy-start.3
  3.9 0.7 %copy-done.3 = s32[2,16,128]{2,1,0:T(8,128)S(1)} copy-done((s32[2,16,128]{2,1,0:T(8,128)S(1)}, s32[2,16,128]{2,1,0:T(8,128)}, u32[]{:S(2)}) %copy-start.3) | copy-done | bytes 16408
  4.6 21.8 %film_and_substrate.1 = (f32[9,2,16,128]{3,2,1,0:T(8,128)S(1)}, f32[3,4,16,128]{3,2,1,0:T(8,128)S(1)}) custom-call(f32[9,2,16,128]{3,2,1,0:T(8,128)S(1)} %copy-done, f32[2,16,128]{2,1,0:T(8,128)S(1)} %copy-done.2, s32[2,16,128]{2,1,0:T(8,128)S(1)} %copy-done.3, f32[3,4,16,128]{3,2,1,0:T(8,128)S(1)} %copy-done.1, s32[16,1]{1,0:T(8,128)S(1)} %copy.8.regions, ...), custom_call_target="tpu_custom_call" | custom-call | tf_op jit(solution)/shard_map/film_and_substrate/pallas_call | solution.py:455
  26.4 0.7 %copy.11 = f32[9,2,16,128]{3,2,1,0:T(8,128)} copy(f32[9,2,16,128]{3,2,1,0:T(8,128)S(1)} %get-tuple-element.4) | data formatting | bytes 294912
  27.1 0.6 %copy.12 = f32[3,4,16,128]{3,2,1,0:T(8,128)} copy(f32[3,4,16,128]{3,2,1,0:T(8,128)S(1)} %get-tuple-element.5) | data formatting | bytes 196608
Async XLA Ops:
  0.6 0.8 %copy-start.4 = (f32[4,4]{1,0:T(4,128)S(1)}, f32[4,4]{1,0:T(4,128)}, u32[]{:S(2)}) copy-start(f32[4,4]{1,0:T(4,128)} %table.1) | copy-start | bytes 196
  1.4 0.9 %copy-start = (f32[9,2,16,128]{3,2,1,0:T(8,128)S(1)}, f32[9,2,16,128]{3,2,1,0:T(8,128)}, u32[]{:S(2)}) copy-start(f32[9,2,16,128]{3,2,1,0:T(8,128)} %wave.1) | copy-start | bytes 442372
  2.3 0.9 %copy-start.1 = (f32[3,4,16,128]{3,2,1,0:T(8,128)S(1)}, f32[3,4,16,128]{3,2,1,0:T(8,128)}, u32[]{:S(2)}) copy-start(f32[3,4,16,128]{3,2,1,0:T(8,128)} %spin.1) | copy-start | bytes 294916
  3.2 0.7 %copy-start.2 = (f32[2,16,128]{2,1,0:T(8,128)S(1)}, f32[2,16,128]{2,1,0:T(8,128)}, u32[]{:S(2)}) copy-start(f32[2,16,128]{2,1,0:T(8,128)} %buoy.1) | copy-start | bytes 49156
  3.9 0.7 %copy-start.3 = (s32[2,16,128]{2,1,0:T(8,128)S(1)}, s32[2,16,128]{2,1,0:T(8,128)}, u32[]{:S(2)}) copy-start(s32[2,16,128]{2,1,0:T(8,128)} %sponge.1) | copy-start | bytes 49156
